TPU v7x, 32 devices: a whole 2x2x4 slice. The times are simulated.
32 devices in a mesh: groups: 2 (over x), ctx: 4 (over y, core), head: 4 (over z).
Axes of the slice: x: 2, y: 2, z: 4, core: 2. Of those that a mesh axis runs over, the one named last changes fastest.
Arguments:
- xs: bfloat16 [12288, 4096], P(('groups', 'ctx', 'head')), parts along dimension 0, may hold values from -6 to 6
- gate_in: bfloat16 [12288, 4096], P(('groups', 'ctx', 'head')), parts along dimension 0, may hold values from -6 to 6
- bc: bfloat16 [12288, 256], P(('groups', 'ctx', 'head')), parts along dimension 0, may hold values from -1.78125 to 1.78125
- dt_raw: bfloat16 [12288, 64], P(('groups', 'ctx', 'head')), parts along dimension 0, may hold values from -4 to 4
- doc_ids: int32 [12288], P(('groups', 'ctx')), parts along dimension 0, may hold values from 0 to 31, never falling along the last dimension, each value on 1 to 3072 neighbouring positions
- dt_bias: float32 [64], P('head'), may hold values from -1 to 1
- decay_rate: float32 [64], P('head'), may hold values from 8.138021e-06 to 0.03
- skip: float32 [64], P('head'), may hold values from 0.5 to 1.5
- norm_gain: float32 [4096], replicated, may hold values from 0.5 to 1.5
Outputs:
- mixed: bfloat16 [12288, 4096], P(('groups', 'ctx', 'head')), parts along dimension 0
There are 2 independent parts, one for each index of `groups`. A program takes and returns all parts, laid end to end along the dimension named above; an argument that names none is the same for every part. Nothing has to cross between parts.
Inputs may be any that keep to these rules, and one draw needn't show every extreme that they name: `doc_ids`: document ids never fall along the window; each document is one run of tokens, at most 3072 long, and one document is exactly that long.
All inputs are finite; a program needn't handle non-finite values.
Results may differ from a plain program's by a relative error of at most 0.007.
Values may be sent and summed in bfloat16 or wider, within the bound.
A program may use at most 64 MiB of HBM per device.

v0:
```python
import jax
import jax.numpy as jnp
from jax import lax
from jax.sharding import PartitionSpec as P

STATE = 128
EXTRA = 16
SPAN_AXES = ("ctx", "head")


def shards(xs, gate_in, bc, dt_raw, doc_ids, dt_bias, decay_rate, skip, norm_gain):
    f32, bf16 = (jnp.float32, jnp.bfloat16)
    tokens, columns = xs.shape
    heads = dt_raw.shape[1]
    hdim = columns // heads
    devices = lax.axis_size("ctx") * lax.axis_size("head")
    own = columns // devices
    params = lax.all_gather(jnp.stack([dt_bias, decay_rate, skip]), "head", axis=1, tiled=True)
    ids = lax.dynamic_slice(doc_ids, (lax.axis_index("head") * tokens,), (tokens,))
    dt = jax.nn.softplus(dt_raw.astype(f32) + params[0][None, :])
    lower = jnp.arange(tokens)[:, None] >= jnp.arange(tokens)[None, :]
    log_decay = -jnp.dot(
        lower.astype(f32), dt * params[1][None, :], precision=lax.Precision.HIGHEST
    )
    log_end = log_decay[-1]
    middle = 0.5 * log_end
    spread = lambda v: jnp.repeat(v, hdim, axis=-1)
    into = jnp.exp(middle[None, :] - log_decay) * dt
    out_of = jnp.exp(log_decay - middle[None, :])
    x = xs.astype(f32)
    weighted = (spread(into) * x).astype(bf16)
    in_b, in_c = (bc[:, :STATE], bc[:, STATE:])
    scores = jnp.einsum("tn,sn->ts", in_c, in_b, preferred_element_type=f32)
    scores = jnp.where(lower & (ids[:, None] == ids[None, :]), scores, 0.0).astype(bf16)
    last_b = jnp.where((ids == ids[-1])[:, None], in_b, jnp.zeros_like(in_b))
    state = jnp.einsum("sn,sq->nq", last_b, weighted, preferred_element_type=f32)
    state = (state * spread(jnp.exp(middle))[None, :]).astype(bf16)
    factor = spread(jnp.exp(log_end))
    factor_hi = factor.astype(bf16)
    factor_lo = (factor - factor_hi.astype(f32)).astype(bf16)
    back = jnp.full((columns,), ids[-1].astype(bf16))
    extra = jnp.concatenate(
        [jnp.stack([factor_hi, factor_lo, back]), jnp.zeros((EXTRA - 3, columns), bf16)]
    )
    block = jnp.concatenate([state, extra])
    block = block.reshape(STATE + EXTRA, devices, own).transpose(1, 0, 2)
    got = lax.all_to_all(block, SPAN_AXES, split_axis=0, concat_axis=0, tiled=True)

    def advance(carry, piece):
        entering, before = carry
        mult = piece[STATE].astype(f32) + piece[STATE + 1].astype(f32)
        back_id = piece[STATE + 2].astype(f32)
        give = jnp.concatenate(
            [entering.astype(bf16), before[None].astype(bf16), jnp.zeros((EXTRA - 1, own), bf16)]
        )
        keep = jnp.where(back_id == before, mult, 0.0)
        return ((keep[None] * entering + piece[:STATE].astype(f32), back_id), give)

    unused, give = lax.scan(
        advance, (jnp.zeros((STATE, own), f32), jnp.full((own,), -1.0, f32)), got
    )
    back_here = lax.all_to_all(give, SPAN_AXES, split_axis=0, concat_axis=0, tiled=True)
    back_here = back_here.transpose(1, 0, 2).reshape(STATE + EXTRA, columns)
    before = back_here[STATE, 0].astype(f32)
    inside_c = jnp.where((ids.astype(f32) == before)[:, None], in_c, jnp.zeros_like(in_c))
    carried = jnp.dot(inside_c, back_here[:STATE], preferred_element_type=f32)
    local = jnp.dot(scores, weighted, preferred_element_type=f32)
    ssm = (
        spread(out_of) * (local + carried * spread(jnp.exp(middle))[None, :])
        + spread(params[2])[None, :] * x
    )
    gated = ssm.astype(bf16).astype(f32) * jax.nn.silu(gate_in.astype(f32))
    scale = lax.rsqrt(jnp.mean(gated * gated, axis=-1, keepdims=True) + 1e-05)
    return (gated * scale * norm_gain[None, :]).astype(bf16)


def solution(mesh):
    rows = P(("groups", "ctx", "head"), None)
    return jax.shard_map(
        shards,
        mesh=mesh,
        in_specs=(
            rows,
            rows,
            rows,
            rows,
            P(("groups", "ctx")),
            P("head"),
            P("head"),
            P("head"),
            P(),
        ),
        out_specs=rows,
        check_vma=False,
    )
```

profile of v0, /device:TPU:0, one launch (start us, length us, event | category | flops | bytes accessed | tf_op | source)
XLA Modules:
  0.0 152.1 jit_solution(1938761750910926963)
XLA Ops:
  0.0 0.8 dynamic_slice.7
  0.8 0.6 slice.52
  1.4 1.4 broadcast_compare_fusion
  3.4 0.7 maximum_bitcast_fusion.1
  4.1 13.5 %all-gather = f32[4,16,3]{1,2,0:T(4,128)S(1)} all-gather(f32[1,16,3]{1,2,0:T(4,128)S(1)} %maximum_bitcast_fusion.1), channel_id=1, replica_groups=mesh['groups'=2,'ctx'=4,'head'=4] {'head'}, dimensions={0}, use_global_device_ids=true | all-gather | bytes 960 | tf_op jit(solution)/shard_map/all_gather | solution.py:18
  17.7 0.1 reshape.110
  17.8 1.3 convolution_negate_fusion
  19.0 0.2 exponential_reduce_fusion
  19.3 0.9 exponential_multiply_fusion
  20.4 3.1 %broadcast_in_dim.69 = f32[384,64,64]{0,2,1:T(8,128)} broadcast(f32[384,64]{0,1:T(8,128)S(1)} %get-tuple-element.66), dimensions={0,1} | broadcast | bytes 6389760 | tf_op jit(solution)/shard_map/broadcast_in_dim | solution.py:27
  23.4 6.8 %copy.20 = f32[384,4096]{1,0:T(8,128)} copy(f32[384,4096]{0,1:T(8,128)} %bitcast.51) | data formatting | bytes 12582912 | tf_op jit(solution)/shard_map/reshape | solution.py:27
  30.2 3.7 %fusion.12 = bf16[128,4096]{1,0:T(8,128)(2,1)S(1)} fusion(f32[4096]{0:T(1024)S(1)} %mul.100, pred[384]{0:T(512)(128)(4,1)S(1)} %broadcast_compare_fusion, bf16[384,256]{1,0:T(8,128)(2,1)S(1)} %copy-done.1, f32[384,4096]{1,0:T(8,128)} %copy.20, bf16[384,4096]{1,0:T(8,128)(2,1)S(1)} %copy-done), kind=kOutput, calls=%fused_computation.27 | convolution fusion | flops 408469504 | bytes 10600960 | tf_op jit(solution)/shard_map/sn,sq->nq/dot_general | solution.py:36
  33.9 0.1 copy.29
  34.0 0.1 exp.34
  34.1 0.1 broadcast_in_dim.75
  34.2 0.1 broadcast_in_dim.76
  34.4 5.4 %concatenate.10 = bf16[144,16,256]{2,0,1:T(8,128)(2,1)} concatenate(bf16[128,16,256]{2,0,1:T(8,128)(2,1)S(1)} %bitcast.55, bf16[1,16,256]{2,0,1:T(2,128)(2,1)S(1)} %get-tuple-element.69, bf16[1,16,256]{2,0,1:T(2,128)(2,1)S(1)} %get-tuple-element.68, bf16[1,16,256]{2,0,1:T(2,128)(2,1)S(1)} %stack_broadcast_in_dim.3, bf16[13,16,256]{2,0,1:T(8,128)(2,1)S(1)} %broadcast_in_dim.77), dimensions={0} | concatenate | bytes 2359296 | tf_op jit(solution)/shard_map/concatenate | solution.py:45
  39.8 4.5 %all-to-all-start = ((bf16[16,144,256]{2,1,0:T(8,128)(2,1)}), bf16[16,144,256]{2,1,0:T(8,128)(2,1)S(1)}, u32[]{:S(2)}, u32[]{:S(2)}) async-start(bf16[16,144,256]{2,1,0:T(8,128)(2,1)} %bitcast.11), calls=%async_computation | async-start | bytes 2359296 | tf_op jit(solution)/shard_map/all_to_all | solution.py:47
  44.2 29.8 %all-to-all-done = bf16[16,144,256]{2,1,0:T(8,128)(2,1)S(1)} async-done(((bf16[16,144,256]{2,1,0:T(8,128)(2,1)}), bf16[16,144,256]{2,1,0:T(8,128)(2,1)S(1)}, u32[]{:S(2)}, u32[]{:S(2)}) %all-to-all-start) | async-done | bytes 1179680 | tf_op jit(solution)/shard_map/all_to_all | solution.py:47
  74.0 15.2 %while.15 = (s32[]{:T(128)}, f32[128,256]{1,0:T(8,128)S(1)}, f32[256]{0:T(256)S(1)}, bf16[16,144,256]{2,1,0:T(8,128)(2,1)}, bf16[16,144,256]{2,1,0:T(8,128)(2,1)...) while((s32[]{:T(128)}, f32[128,256]{1,0:T(8,128)S(1)}, ...), condition=%wide.region_1.2_spmd.clone, body=%wide.region_0.1_spmd.clone.sunk | while | flops 386822 | bytes 677192 | solution.py:59
  74.2 0.1 pad.2.clone.2
  74.2 0.7 fusion.57
  75.1 0.1 pad.2.clone.2
  75.2 0.7 fusion.57
  76.1 0.1 pad.2.clone.2
  76.1 0.7 fusion.57
  77.0 0.1 pad.2.clone.2
  77.1 0.7 fusion.57
  78.0 0.1 pad.2.clone.2
  78.0 0.7 fusion.57
  78.9 0.1 pad.2.clone.2
  79.0 0.7 fusion.57
  79.9 0.1 pad.2.clone.2
  79.9 0.7 fusion.57
  80.8 0.1 pad.2.clone.2
  80.9 0.7 fusion.57
  81.8 0.1 pad.2.clone.2
  81.9 0.7 fusion.57
  82.7 0.1 pad.2.clone.2
  82.8 0.7 fusion.57
  83.7 0.1 pad.2.clone.2
  83.8 0.7 fusion.57
  84.6 0.1 pad.2.clone.2
  84.7 0.7 fusion.57
  85.6 0.1 pad.2.clone.2
  85.7 0.7 fusion.57
  86.5 0.1 pad.2.clone.2
  86.6 0.7 fusion.57
  87.5 0.1 pad.2.clone.2
  87.6 0.7 fusion.57
  88.4 0.1 pad.2.clone.2
  88.5 0.7 fusion.57
  89.2 3.7 %all-to-all-start.1 = ((bf16[16,144,256]{2,1,0:T(8,128)(2,1)}), bf16[16,144,256]{2,1,0:T(8,128)(2,1)S(1)}, u32[]{:S(2)}, u32[]{:S(2)}) async-start(bf16[16,144,256]{2,1,0:T(8,128)(2,1)} %get-tuple-element.32), calls=%async_computation.1 | async-start | bytes 2359296 | tf_op jit(solution)/shard_map/all_to_all | solution.py:62
  93.1 3.0 %broadcast_in_dim.67 = f32[384,64,64]{0,2,1:T(8,128)} broadcast(f32[384,64]{0,1:T(8,128)S(1)} %get-tuple-element.67), dimensions={0,1} | broadcast | bytes 6389760 | tf_op jit(solution)/shard_map/broadcast_in_dim | solution.py:27
  96.1 6.7 %copy.24 = f32[384,4096]{1,0:T(8,128)} copy(f32[384,4096]{0,1:T(8,128)} %bitcast.52) | data formatting | bytes 12582912 | tf_op jit(solution)/shard_map/reshape | solution.py:27
  102.8 19.9 %all-to-all-done.1 = bf16[16,144,256]{2,1,0:T(8,128)(2,1)S(1)} async-done(((bf16[16,144,256]{2,1,0:T(8,128)(2,1)}), bf16[16,144,256]{2,1,0:T(8,128)(2,1)S(1)}, u32[]{:S(2)}, u32[]{:S(2)}) %all-to-all-start.1) | async-done | bytes 1179680 | tf_op jit(solution)/shard_map/all_to_all | solution.py:62
  122.7 1.6 %copy.22 = bf16[16,144,256]{1,2,0:T(8,128)(2,1)S(1)} copy(bf16[16,144,256]{2,1,0:T(8,128)(2,1)S(1)} %all-to-all-done.1) | data formatting | bytes 2359296 | tf_op jit(solution)/shard_map/all_to_all | solution.py:62
  124.3 1.2 slice.63
  125.5 0.1 copy.27
  125.6 0.6 slice.62
  126.9 0.8 convert_compare_fusion
  127.6 4.8 %fusion.20 = f32[384,4096]{1,0:T(8,128)} fusion(bf16[128,4096]{0,1:T(8,128)(2,1)} %bitcast.56, pred[384]{0:T(512)(128)(4,1)S(1)} %convert_compare_fusion, bf16[384,256]{1,0:T(8,128)(2,1)S(1)} %copy-done.1), kind=kOutput, calls=%fused_computation.39 | convolution fusion | flops 402702336 | bytes 7438848 | tf_op jit(solution)/shard_map/dot_general | solution.py:66
  132.5 14.2 %multiply_reduce_fusion = (f32[384]{0:T(512)S(1)}, f32[384,4096]{1,0:T(8,128)}) fusion(bf16[384,4096]{1,0:T(8,128)(2,1)} %param.12, bf16[384,4096]{1,0:T(8,128)(2,1)} %param.11, f32[4096]{0:T(1024)S(1)} %mul.106, f32[384,4096]{1,0:T(8,128)} %copy.24, f32[384,4096]{1,0:T(8,128)} %fusion.20, f32[4096]{0:T(1024)S(1)} %mul.100, f32[384,4096]{1,0:T(8,128)} %copy.20, ...), kind=kOutput, calls=%fused_computation.25 | convolution fusion | flops 1276329600 | bytes 34838016 | tf_op jit(solution)/shard_map/dot_general | solution.py:67
  146.7 5.4 %multiply_convert_fusion = bf16[384,4096]{1,0:T(8,128)(2,1)} fusion(f32[384,4096]{1,0:T(8,128)} %get-tuple-element.74, f32[4096]{0:T(1024)S(1)} %copy-done.2, f32[384]{0:T(512)S(1)} %add_rsqrt_fusion), kind=kLoop, calls=%fused_computation.24 | loop fusion | flops 4718592 | bytes 9455104 | tf_op jit(solution)/shard_map/convert_element_type | solution.py:74
  (147 shorter events, 2.0 us)
Async XLA Ops:
  23.4 6.8 %copy-start = (bf16[384,4096]{1,0:T(8,128)(2,1)S(1)}, bf16[384,4096]{1,0:T(8,128)(2,1)}, u32[]{:S(2)}) copy-start(bf16[384,4096]{1,0:T(8,128)(2,1)} %param.11) | copy-start | bytes 9437188
  23.4 6.8 %copy-start.1 = (bf16[384,256]{1,0:T(8,128)(2,1)S(1)}, bf16[384,256]{1,0:T(8,128)(2,1)}, u32[]{:S(2)}) copy-start(bf16[384,256]{1,0:T(8,128)(2,1)} %param.13) | copy-start | bytes 589828
  39.8 34.2 %all-to-all-start = ((bf16[16,144,256]{2,1,0:T(8,128)(2,1)}), bf16[16,144,256]{2,1,0:T(8,128)(2,1)S(1)}, u32[]{:S(2)}, u32[]{:S(2)}) async-start(bf16[16,144,256]{2,1,0:T(8,128)(2,1)} %bitcast.11), calls=%async_computation | async-start | bytes 2359296 | tf_op jit(solution)/shard_map/all_to_all | solution.py:47
  89.2 33.4 %all-to-all-start.1 = ((bf16[16,144,256]{2,1,0:T(8,128)(2,1)}), bf16[16,144,256]{2,1,0:T(8,128)(2,1)S(1)}, u32[]{:S(2)}, u32[]{:S(2)}) async-start(bf16[16,144,256]{2,1,0:T(8,128)(2,1)} %get-tuple-element.32), calls=%async_computation.1 | async-start | bytes 2359296 | tf_op jit(solution)/shard_map/all_to_all | solution.py:62
  132.5 14.2 %copy-start.2 = (f32[4096]{0:T(1024)S(1)}, f32[4096]{0:T(1024)}, u32[]{:S(2)}) copy-start(f32[4096]{0:T(1024)} %param.19) | copy-start | bytes 49156
where the time goes:
time: 153 us; the launch traced here: 152 us
  waiting for transfers between devices  49.7 us (32%)
  local copies, waits for them, and re-layouts  31.9 us (21%)
  matrix products  24 us (16%)
  other arithmetic  22.5 us (15%)
  blocking collectives  13.5 us (9%)
  starting transfers between devices  8.15 us (5%)
    all_to_all x1, waiting for transfers between devices, shards(): lax.all_to_all(block, SPAN_AXES, split_axis=0, concat_axis=0, tiled=True)  29.8 us
    all_to_all x1, waiting for transfers between devices, shards(): lax.all_to_all(give, SPAN_AXES, split_axis=0, concat_axis=0, tiled=True)  19.9 us
    dot_general x1, matrix products, shards(): local = jnp.dot(scores, weighted, preferred_element_type=f32)  14.2 us
    all_gather x1, blocking collectives, shards(): lax.all_gather(jnp.stack([dt_bias, decay_rate, skip]), 'head', axis=1, ti...  13.5 us
    reshape x2, local copies, waits for them, and re-layouts, shards(): spread = lambda v: jnp.repeat(v, hdim, axis=-1)  13.4 us
    dynamic_update_slice x16, other arithmetic, shards(): lax.scan(advance, (jnp.zeros((STATE, own), f32), jnp.full((own,), -1.0, f...  11.6 us
    broadcast_in_dim x6, local copies, waits for them, and re-layouts, shards(): spread = lambda v: jnp.repeat(v, hdim, axis=-1)  6.4 us
    concatenate x2, local copies, waits for them, and re-layouts, shards(): block = jnp.concatenate([state, extra])  5.48 us
  transfers between devices with their start and end apart: 2, of which 2 were waited for; matrix products, arithmetic and copies ran while one was open for 6% of the time, Pallas kernels for 0%

commit v1 on v0

--- a/solution.py
+++ b/solution.py
@@ -8,6 +8,27 @@
 SPAN_AXES = ("ctx", "head")
 
 
+def divide_modes(target, along_axis):
+    known, d_next, e_next = (
+        lax.psum(1, axis_name=along_axis),
+        lax.axis_index(along_axis),
+        target.shape[1],
+    )
+    rack = []
+    for no, h in enumerate(target.shape):
+        rack.append(h * known if no == 1 else h)
+    w1 = lax.dynamic_update_slice_in_dim(
+        jnp.zeros(rack, target.dtype), target, d_next * e_next, axis=1
+    )
+    for pp in range(1, known):
+        series = []
+        for no in range(known):
+            series.append((no, (no + 1) % known))
+        target = lax.ppermute(target, axis_name=along_axis, perm=series)
+        w1 = lax.dynamic_update_slice_in_dim(w1, target, (d_next - pp) % known * e_next, axis=1)
+    return w1
+
+
 def shards(xs, gate_in, bc, dt_raw, doc_ids, dt_bias, decay_rate, skip, norm_gain):
     f32, bf16 = (jnp.float32, jnp.bfloat16)
     tokens, columns = xs.shape
@@ -15,7 +36,7 @@
     hdim = columns // heads
     devices = lax.axis_size("ctx") * lax.axis_size("head")
     own = columns // devices
-    params = lax.all_gather(jnp.stack([dt_bias, decay_rate, skip]), "head", axis=1, tiled=True)
+    params = divide_modes(jnp.stack([dt_bias, decay_rate, skip]), along_axis="head")
     ids = lax.dynamic_slice(doc_ids, (lax.axis_index("head") * tokens,), (tokens,))
     dt = jax.nn.softplus(dt_raw.astype(f32) + params[0][None, :])
     lower = jnp.arange(tokens)[:, None] >= jnp.arange(tokens)[None, :]

time: 153 us -> 152 us (level)
  blocking collectives: 13.5 us -> 0 us
  waiting for transfers between devices: 49.7 us -> 58.7 us
  starting transfers between devices: 8.15 us -> 12 us
    all_gather x1 -> x0, blocking collectives: 13.5 us -> none  [shards(): lax.all_gather(jnp.stack([dt_bias, decay_rate, skip]), 'head', axis=1, ti...]
    ppermute x0 -> x3, waiting for transfers between devices: none -> 8.93 us  [divide_modes(): target = lax.ppermute(target, axis_name=along_axis, perm=series)]
    ppermute x0 -> x3, starting transfers between devices: none -> 4.55 us  [divide_modes(): target = lax.ppermute(target, axis_name=along_axis, perm=series)]
  transfers between devices with their start and end apart: 2 -> 5, of which waited for: 2 -> 5; matrix products, arithmetic and copies ran while one was open for 6% -> 9% of each run, Pallas kernels for 0% -> 0%
where the time goes in v1:
time: 152 us; the launch traced here: 151 us
  waiting for transfers between devices  58.7 us (39%)
  local copies, waits for them, and re-layouts  32.2 us (21%)
  matrix products  23.9 us (16%)
  other arithmetic  22.5 us (15%)
  starting transfers between devices  12 us (8%)
    all_to_all x1, waiting for transfers between devices, shards(): lax.all_to_all(block, SPAN_AXES, split_axis=0, concat_axis=0, tiled=True)  29.7 us
    all_to_all x1, waiting for transfers between devices, shards(): lax.all_to_all(give, SPAN_AXES, split_axis=0, concat_axis=0, tiled=True)  20 us
    dot_general x1, matrix products, shards(): local = jnp.dot(scores, weighted, preferred_element_type=f32)  14.1 us
    reshape x2, local copies, waits for them, and re-layouts, shards(): spread = lambda v: jnp.repeat(v, hdim, axis=-1)  13.3 us
    dynamic_update_slice x16, other arithmetic, shards(): lax.scan(advance, (jnp.zeros((STATE, own), f32), jnp.full((own,), -1.0, f...  11.6 us
    ppermute x3, waiting for transfers between devices, divide_modes(): target = lax.ppermute(target, axis_name=along_axis, perm=series)  8.93 us
    broadcast_in_dim x6, local copies, waits for them, and re-layouts, shards(): spread = lambda v: jnp.repeat(v, hdim, axis=-1)  6.38 us
    concatenate x2, local copies, waits for them, and re-layouts, shards(): block = jnp.concatenate([state, extra])  5.48 us
  transfers between devices with their start and end apart: 5, of which 5 were waited for; matrix products, arithmetic and copies ran while one was open for 9% of the time, Pallas kernels for 0%

profile of v1, /device:TPU:0, one launch (start us, length us, event | category | flops | bytes accessed | tf_op | source)
XLA Modules:
  0.0 151.5 jit_solution(5026727425285963729)
XLA Ops:
  0.0 0.7 pad_maximum_fusion
  0.7 3.1 %collective-permute-start = (f32[3,16]{1,0:T(4,128)S(1)}, f32[3,16]{1,0:T(4,128)S(1)}, u32[]{:S(2)}, u32[]{:S(2)}) collective-permute-start(f32[3,16]{1,0:T(4,128)S(1)} %pad_maximum_fusion), channel_id=1, source_target_pairs={{0,1},{1,2},{2,3},{3,0},{4,5},{5,6},{6,7},{7,4},{8,9},{9,10},{10,1... | collective-permute-start | bytes 584 | tf_op jit(solution)/shard_map/ppermute | solution.py:27
  3.8 0.8 dynamic_slice.7
  4.5 0.6 slice.52
  5.1 1.4 broadcast_compare_fusion
  7.2 0.2 collective-permute-done
  7.3 1.5 collective-permute-start.1
  8.9 3.8 %collective-permute-done.1 = f32[3,16]{1,0:T(4,128)S(1)} collective-permute-done((f32[3,16]{1,0:T(4,128)S(1)}, f32[3,16]{1,0:T(4,128)S(1)}, u32[]{:S(2)}, u32[]{:S(2)}) %collective-permute-start.1) | collective-permute-done | bytes 224 | tf_op jit(solution)/shard_map/ppermute | solution.py:27
  12.7 0.2 dynamic_update_slice.17
  12.9 0.2 dynamic_update_slice.18
  13.1 5.0 %collective-permute-done.2 = f32[3,16]{1,0:T(4,128)S(1)} collective-permute-done((f32[3,16]{1,0:T(4,128)S(1)}, f32[3,16]{1,0:T(4,128)S(1)}, u32[]{:S(2)}, u32[]{:S(2)}) %collective-permute-start.2) | collective-permute-done | bytes 224 | tf_op jit(solution)/shard_map/ppermute | solution.py:27
  18.1 0.2 dynamic_update_slice.19
  18.3 1.3 convolution_negate_fusion
  19.6 0.2 exponential_reduce_fusion
  19.8 0.9 exponential_multiply_fusion
  20.9 3.1 %broadcast_in_dim.73 = f32[384,64,64]{0,2,1:T(8,128)} broadcast(f32[384,64]{0,1:T(8,128)S(1)} %get-tuple-element.66), dimensions={0,1} | broadcast | bytes 6389760 | tf_op jit(solution)/shard_map/broadcast_in_dim | solution.py:48
  24.0 6.7 %copy.18 = f32[384,4096]{1,0:T(8,128)} copy(f32[384,4096]{0,1:T(8,128)} %bitcast.44) | data formatting | bytes 12582912 | tf_op jit(solution)/shard_map/reshape | solution.py:48
  30.7 3.7 %fusion.12 = bf16[128,4096]{1,0:T(8,128)(2,1)S(1)} fusion(f32[4096]{0:T(1024)S(1)} %mul.116, pred[384]{0:T(512)(128)(4,1)S(1)} %broadcast_compare_fusion, bf16[384,256]{1,0:T(8,128)(2,1)S(1)} %copy-done.1, f32[384,4096]{1,0:T(8,128)} %copy.18, bf16[384,4096]{1,0:T(8,128)(2,1)S(1)} %copy-done), kind=kOutput, calls=%fused_computation.27 | convolution fusion | flops 408469504 | bytes 10600960 | tf_op jit(solution)/shard_map/sn,sq->nq/dot_general | solution.py:57
  34.4 0.1 copy.27
  34.5 0.1 exp.34
  34.6 0.1 broadcast_in_dim.79
  34.7 0.1 broadcast_in_dim.80
  34.9 5.4 %concatenate.10 = bf16[144,16,256]{2,0,1:T(8,128)(2,1)} concatenate(bf16[128,16,256]{2,0,1:T(8,128)(2,1)S(1)} %bitcast.48, bf16[1,16,256]{2,0,1:T(2,128)(2,1)S(1)} %get-tuple-element.69, bf16[1,16,256]{2,0,1:T(2,128)(2,1)S(1)} %get-tuple-element.68, bf16[1,16,256]{2,0,1:T(2,128)(2,1)S(1)} %stack_broadcast_in_dim.3, bf16[13,16,256]{2,0,1:T(8,128)(2,1)S(1)} %broadcast_in_dim.81), dimensions={0} | concatenate | bytes 2359296 | tf_op jit(solution)/shard_map/concatenate | solution.py:66
  40.3 3.7 %all-to-all-start = ((bf16[16,144,256]{2,1,0:T(8,128)(2,1)}), bf16[16,144,256]{2,1,0:T(8,128)(2,1)S(1)}, u32[]{:S(2)}, u32[]{:S(2)}) async-start(bf16[16,144,256]{2,1,0:T(8,128)(2,1)} %bitcast.8), calls=%async_computation | async-start | bytes 2359296 | tf_op jit(solution)/shard_map/all_to_all | solution.py:68
  44.0 29.7 %all-to-all-done = bf16[16,144,256]{2,1,0:T(8,128)(2,1)S(1)} async-done(((bf16[16,144,256]{2,1,0:T(8,128)(2,1)}), bf16[16,144,256]{2,1,0:T(8,128)(2,1)S(1)}, u32[]{:S(2)}, u32[]{:S(2)}) %all-to-all-start) | async-done | bytes 1179680 | tf_op jit(solution)/shard_map/all_to_all | solution.py:68
  73.7 15.2 %while.15 = (s32[]{:T(128)}, f32[128,256]{1,0:T(8,128)S(1)}, f32[256]{0:T(256)S(1)}, bf16[16,144,256]{2,1,0:T(8,128)(2,1)}, bf16[16,144,256]{2,1,0:T(8,128)(2,1)...) while((s32[]{:T(128)}, f32[128,256]{1,0:T(8,128)S(1)}, ...), condition=%wide.region_1.2_spmd.clone, body=%wide.region_0.1_spmd.clone.sunk | while | flops 386822 | bytes 677192 | solution.py:80
  73.9 0.1 pad.2.clone.2
  74.0 0.7 fusion.57
  74.8 0.1 pad.2.clone.2
  74.9 0.7 fusion.57
  75.9 0.7 fusion.57
  76.8 0.7 fusion.57
  77.8 0.7 fusion.57
  78.7 0.7 fusion.57
  79.7 0.7 fusion.57
  80.6 0.7 fusion.57
  81.5 0.1 pad.2.clone.2
  81.6 0.7 fusion.57
  82.4 0.1 pad.2.clone.2
  82.5 0.7 fusion.57
  83.4 0.1 pad.2.clone.2
  83.5 0.7 fusion.57
  84.3 0.1 pad.2.clone.2
  84.4 0.7 fusion.57
  85.3 0.1 pad.2.clone.2
  85.4 0.7 fusion.57
  86.2 0.1 pad.2.clone.2
  86.3 0.7 fusion.57
  87.2 0.1 pad.2.clone.2
  87.3 0.7 fusion.57
  88.2 0.1 pad.2.clone.2
  88.2 0.7 fusion.57
  89.0 3.7 %all-to-all-start.1 = ((bf16[16,144,256]{2,1,0:T(8,128)(2,1)}), bf16[16,144,256]{2,1,0:T(8,128)(2,1)S(1)}, u32[]{:S(2)}, u32[]{:S(2)}) async-start(bf16[16,144,256]{2,1,0:T(8,128)(2,1)} %get-tuple-element.32), calls=%async_computation.1 | async-start | bytes 2359296 | tf_op jit(solution)/shard_map/all_to_all | solution.py:83
  92.8 3.0 %broadcast_in_dim.71 = f32[384,64,64]{0,2,1:T(8,128)} broadcast(f32[384,64]{0,1:T(8,128)S(1)} %get-tuple-element.67), dimensions={0,1} | broadcast | bytes 6389760 | tf_op jit(solution)/shard_map/broadcast_in_dim | solution.py:48
  95.8 6.5 %copy.22 = f32[384,4096]{1,0:T(8,128)} copy(f32[384,4096]{0,1:T(8,128)} %bitcast.45) | data formatting | bytes 12582912 | tf_op jit(solution)/shard_map/reshape | solution.py:48
  102.4 20.0 %all-to-all-done.1 = bf16[16,144,256]{2,1,0:T(8,128)(2,1)S(1)} async-done(((bf16[16,144,256]{2,1,0:T(8,128)(2,1)}), bf16[16,144,256]{2,1,0:T(8,128)(2,1)S(1)}, u32[]{:S(2)}, u32[]{:S(2)}) %all-to-all-start.1) | async-done | bytes 1179680 | tf_op jit(solution)/shard_map/all_to_all | solution.py:83
  122.4 1.6 %copy.20 = bf16[16,144,256]{1,2,0:T(8,128)(2,1)S(1)} copy(bf16[16,144,256]{2,1,0:T(8,128)(2,1)S(1)} %all-to-all-done.1) | data formatting | bytes 2359296 | tf_op jit(solution)/shard_map/all_to_all | solution.py:83
  124.0 1.2 slice.63
  125.2 0.1 copy.25
  125.3 0.5 slice.62
  126.3 0.8 convert_compare_fusion
  127.1 4.8 %fusion.20 = f32[384,4096]{1,0:T(8,128)} fusion(bf16[128,4096]{0,1:T(8,128)(2,1)} %bitcast.49, pred[384]{0:T(512)(128)(4,1)S(1)} %convert_compare_fusion, bf16[384,256]{1,0:T(8,128)(2,1)S(1)} %copy-done.1), kind=kOutput, calls=%fused_computation.39 | convolution fusion | flops 402702336 | bytes 7438848 | tf_op jit(solution)/shard_map/dot_general | solution.py:87
  132.0 14.1 %multiply_reduce_fusion = (f32[384]{0:T(512)S(1)}, f32[384,4096]{1,0:T(8,128)}) fusion(bf16[384,4096]{1,0:T(8,128)(2,1)} %param.12, bf16[384,4096]{1,0:T(8,128)(2,1)} %param.11, f32[4096]{0:T(1024)S(1)} %mul.122, f32[384,4096]{1,0:T(8,128)} %copy.22, f32[384,4096]{1,0:T(8,128)} %fusion.20, f32[4096]{0:T(1024)S(1)} %mul.116, f32[384,4096]{1,0:T(8,128)} %copy.18, ...), kind=kOutput, calls=%fused_computation.25 | convolution fusion | flops 1276329600 | bytes 34838016 | tf_op jit(solution)/shard_map/dot_general | solution.py:88
  146.0 5.4 %multiply_convert_fusion = bf16[384,4096]{1,0:T(8,128)(2,1)} fusion(f32[384,4096]{1,0:T(8,128)} %get-tuple-element.74, f32[4096]{0:T(1024)S(1)} %copy-done.2, f32[384]{0:T(512)S(1)} %add_rsqrt_fusion), kind=kLoop, calls=%fused_computation.24 | loop fusion | flops 4718592 | bytes 9455104 | tf_op jit(solution)/shard_map/convert_element_type | solution.py:95
  (155 shorter events, 2.5 us)
Async XLA Ops:
  0.7 6.7 %collective-permute-start = (f32[3,16]{1,0:T(4,128)S(1)}, f32[3,16]{1,0:T(4,128)S(1)}, u32[]{:S(2)}, u32[]{:S(2)}) collective-permute-start(f32[3,16]{1,0:T(4,128)S(1)} %pad_maximum_fusion), channel_id=1, source_target_pairs={{0,1},{1,2},{2,3},{3,0},{4,5},{5,6},{6,7},{7,4},{8,9},{9,10},{10,1... | collective-permute-start | bytes 584 | tf_op jit(solution)/shard_map/ppermute | solution.py:27
  7.3 5.4 %collective-permute-start.1 = (f32[3,16]{1,0:T(4,128)S(1)}, f32[3,16]{1,0:T(4,128)S(1)}, u32[]{:S(2)}, u32[]{:S(2)}) collective-permute-start(f32[3,16]{1,0:T(4,128)S(1)} %collective-permute-done), channel_id=1, source_target_pairs={{0,1},{1,2},{2,3},{3,0},{4,5},{5,6},{6,7},{7,4},{8,9},{9,10},{10,1... | collective-permute-start | bytes 584 | tf_op jit(solution)/shard_map/ppermute | solution.py:27
  12.7 5.4 %collective-permute-start.2 = (f32[3,16]{1,0:T(4,128)S(1)}, f32[3,16]{1,0:T(4,128)S(1)}, u32[]{:S(2)}, u32[]{:S(2)}) collective-permute-start(f32[3,16]{1,0:T(4,128)S(1)} %collective-permute-done.1), channel_id=1, source_target_pairs={{0,1},{1,2},{2,3},{3,0},{4,5},{5,6},{6,7},{7,4},{8,9},{9,10},{10,1... | collective-permute-start | bytes 584 | tf_op jit(solution)/shard_map/ppermute | solution.py:27
  24.0 6.7 %copy-start = (bf16[384,4096]{1,0:T(8,128)(2,1)S(1)}, bf16[384,4096]{1,0:T(8,128)(2,1)}, u32[]{:S(2)}) copy-start(bf16[384,4096]{1,0:T(8,128)(2,1)} %param.11) | copy-start | bytes 9437188
  24.0 6.7 %copy-start.1 = (bf16[384,256]{1,0:T(8,128)(2,1)S(1)}, bf16[384,256]{1,0:T(8,128)(2,1)}, u32[]{:S(2)}) copy-start(bf16[384,256]{1,0:T(8,128)(2,1)} %param.13) | copy-start | bytes 589828
  40.3 33.4 %all-to-all-start = ((bf16[16,144,256]{2,1,0:T(8,128)(2,1)}), bf16[16,144,256]{2,1,0:T(8,128)(2,1)S(1)}, u32[]{:S(2)}, u32[]{:S(2)}) async-start(bf16[16,144,256]{2,1,0:T(8,128)(2,1)} %bitcast.8), calls=%async_computation | async-start | bytes 2359296 | tf_op jit(solution)/shard_map/all_to_all | solution.py:68
  89.0 33.4 %all-to-all-start.1 = ((bf16[16,144,256]{2,1,0:T(8,128)(2,1)}), bf16[16,144,256]{2,1,0:T(8,128)(2,1)S(1)}, u32[]{:S(2)}, u32[]{:S(2)}) async-start(bf16[16,144,256]{2,1,0:T(8,128)(2,1)} %get-tuple-element.32), calls=%async_computation.1 | async-start | bytes 2359296 | tf_op jit(solution)/shard_map/all_to_all | solution.py:83
  132.0 14.1 %copy-start.2 = (f32[4096]{0:T(1024)S(1)}, f32[4096]{0:T(1024)}, u32[]{:S(2)}) copy-start(f32[4096]{0:T(1024)} %param.19) | copy-start | bytes 49156
